TPU v7x, 512 devices: a whole 4x8x8 slice. The times are simulated.
512 devices in a mesh: lon: 32 (over x, z_hi, core), lat: 16 (over y, z_lo).
Axes of the slice: x: 4, y: 8, z: 8 (z_hi: 4, z_lo: 2; z = z_hi * 2 + z_lo), core: 2. Of those that a mesh axis runs over, the one named last changes fastest.
Arguments:
- fields: bfloat16 [1, 64, 256, 4096], P(None, None, 'lat', 'lon'), may hold values from -6 to 6
- cotangent: bfloat16 [1, 64, 256, 4096], P(None, None, 'lat', 'lon'), may hold values from -6 to 6
- ocean_mask: int32 [256, 4096], P('lat', 'lon'), may hold values 0 or 1
- seam_partner: int32 [4096], replicated, may hold values from 0 to 4095, as said below
- depth_weight: bfloat16 [64, 7, 7], replicated, may hold values from -0.875 to 0.875
- norm_gain: bfloat16 [64], replicated, may hold values from 0.5 to 1.5
- layer_norm_bias: bfloat16 [64], replicated, may hold values from -3 to 3
- up_weight: bfloat16 [256, 64], replicated, may hold values from -0.75 to 0.75
- up_bias: bfloat16 [256], replicated, may hold values from -3 to 3
- down_weight: bfloat16 [64, 256], replicated, may hold values from -0.375 to 0.375
- layer_scale: bfloat16 [64], replicated, may hold values from 0.5 to 1.5
Outputs:
- output: bfloat16 [1, 64, 256, 4096], P(None, None, 'lat', 'lon')
- grad_fields: bfloat16 [1, 64, 256, 4096], P(None, None, 'lat', 'lon')
- grad_depth: float32 [64, 7, 7], replicated
- grad_gain: float32 [64], replicated
- grad_bias: float32 [64], replicated
- grad_up_weight: float32 [256, 64], replicated
- grad_up_bias: float32 [256], replicated
- grad_down_weight: float32 [64, 256], replicated
- grad_scale: float32 [64], replicated
Inputs may be any that keep to these rules, and one draw needn't show every extreme that they name: seam_partner[i] = (s - i) mod 4096 for one whole number s, so it is its own inverse.
All inputs are finite; a program needn't handle non-finite values. No bound on the sum of `ocean_mask` on one device may be relied on, other than what follows from the above.
Results may differ from a plain program's by a relative error of at most 0.0068.
Values may be sent and summed in bfloat16 or wider, within the bound.
A program may use at most 64 MiB of HBM per device.

v0:
```python
import math
import jax
import jax.numpy as jnp
from jax import lax
from jax.sharding import PartitionSpec as P


def extended_2(cells, sides, width, closed):
    for axis, dim in sides:
        count = lax.axis_size(axis)
        ends = count if closed else count - 1
        head = lax.slice_in_dim(cells, 0, width, axis=dim)
        tail = lax.slice_in_dim(cells, cells.shape[dim] - width, cells.shape[dim], axis=dim)
        cells = jnp.concatenate(
            [
                lax.ppermute(tail, axis, [(i, (i + 1) % count) for i in range(ends)]),
                cells,
                lax.ppermute(head, axis, [((i + 1) % count, i) for i in range(ends)]),
            ],
            axis=dim,
        )
    return cells


def gelu_slope(pre):
    cdf = 0.5 * (1.0 + lax.erf(pre / math.sqrt(2.0)))
    return cdf + pre * jnp.exp(-0.5 * pre * pre) / math.sqrt(2.0 * math.pi)


def cell_terms(
    conv, field, cot, mask, norm_gain, layer_norm_bias, up_weight, up_bias, down_weight, layer_scale
):
    mean_c = jnp.mean(conv, axis=0, keepdims=True)
    centered_input = conv - mean_c
    var_c = jnp.mean(centered_input * centered_input, axis=0, keepdims=True)
    reciprocal_deviation = lax.rsqrt(var_c + 1e-06)
    standardized_input = centered_input * reciprocal_deviation
    layer_norm_gain = norm_gain.astype(jnp.float32)[:, None]
    normalized_output = (
        standardized_input * layer_norm_gain + layer_norm_bias.astype(jnp.float32)[:, None]
    ).astype(jnp.bfloat16)
    pre = (
        jnp.dot(up_weight, normalized_output, preferred_element_type=jnp.float32)
        + up_bias.astype(jnp.float32)[:, None]
    )
    hidden = jax.nn.gelu(pre, approximate=False).astype(jnp.bfloat16)
    branch = jnp.dot(down_weight, hidden, preferred_element_type=jnp.float32)
    scale = layer_scale.astype(jnp.float32)[:, None]
    out = (mask * (field.astype(jnp.float32) + scale * branch)).astype(jnp.bfloat16)
    grad_in = mask * cot.astype(jnp.float32)
    d_branch = (grad_in * scale).astype(jnp.bfloat16)
    g_scale = jnp.sum(grad_in * branch, axis=1)
    contract_cells = (((1,), (1,)), ((), ()))
    contract_first = (((0,), (0,)), ((), ()))
    g_down = lax.dot_general(d_branch, hidden, contract_cells, preferred_element_type=jnp.float32)
    d_hidden = lax.dot_general(
        down_weight, d_branch, contract_first, preferred_element_type=jnp.float32
    )
    d_pre = (d_hidden * gelu_slope(pre)).astype(jnp.bfloat16)
    g_up_b = jnp.sum(d_pre.astype(jnp.float32), axis=1)
    g_up_w = lax.dot_general(
        d_pre, normalized_output, contract_cells, preferred_element_type=jnp.float32
    )
    normalized_gradient = lax.dot_general(
        up_weight, d_pre, contract_first, preferred_element_type=jnp.float32
    )
    gain_gradient = jnp.sum(normalized_gradient * standardized_input, axis=1)
    g_bias = jnp.sum(normalized_gradient, axis=1)
    gradient_through_norm = normalized_gradient * layer_norm_gain
    convolution_gradient = reciprocal_deviation * (
        gradient_through_norm
        - jnp.mean(gradient_through_norm, axis=0, keepdims=True)
        - standardized_input
        * jnp.mean(gradient_through_norm * standardized_input, axis=0, keepdims=True)
    )
    return (
        out,
        convolution_gradient.astype(jnp.bfloat16),
        (gain_gradient, g_bias, g_up_w, g_up_b, g_down, g_scale),
    )


def make_picker(wanted, carry, piece):
    width = piece.shape[3]
    inside = (wanted >= 0) & (wanted < width)
    picked = jnp.take(piece, jnp.clip(wanted, 0, width - 1), axis=3)
    return jnp.where(inside[None, None, None, :], picked, carry)


def shards(
    fields,
    cotangent,
    ocean_mask,
    seam_partner,
    depth_weight,
    norm_gain,
    layer_norm_bias,
    up_weight,
    up_bias,
    down_weight,
    layer_scale,
):
    samples, chans, rows, cols = fields.shape
    total_lon = seam_partner.shape[0]
    lon_start = lax.axis_index("lon") * cols
    positions = (lon_start + jnp.arange(-3, cols + 3, dtype=jnp.int32)) % total_lon
    partner_cols = jnp.take(seam_partner, positions)
    own_partner = partner_cols[3 : cols + 3]
    is_top = lax.axis_index("lat") == lax.axis_size("lat") - 1
    weight_f = depth_weight.astype(jnp.float32)
    mask_f = ocean_mask.astype(jnp.float32)
    lon_padded = extended_2(fields, (("lon", 3),), 3, True)
    banded = extended_2(lon_padded, (("lat", 2),), 3, False)
    upper = fields[:, :, rows - 3 :, :][:, :, ::-1, :]
    fold_init = jnp.zeros((samples, chans, 3, cols + 6), jnp.bfloat16)
    folded = make_picker(partner_cols, fold_init, lax.all_gather(upper, "lon", axis=3, tiled=True))
    top_rows = jnp.where(is_top, folded, banded[:, :, rows + 3 :, :])
    extended = jnp.concatenate([banded[:, :, : rows + 3, :], top_rows], axis=2)
    conv = jnp.zeros((samples, chans, rows, cols), jnp.float32)
    for row_tap in range(7):
        for col_tap in range(7):
            conv = conv + weight_f[:, row_tap, col_tap][None, :, None, None] * extended[
                :, :, row_tap : row_tap + rows, col_tap : col_tap + cols
            ].astype(jnp.float32)
    mask_flat = mask_f.reshape(1, rows * cols)
    out_s, dconv_s, parts = cell_terms(
        conv[0].reshape(chans, rows * cols),
        fields[0].reshape(chans, rows * cols),
        cotangent[0].reshape(chans, rows * cols),
        mask_flat,
        norm_gain,
        layer_norm_bias,
        up_weight,
        up_bias,
        down_weight,
        layer_scale,
    )
    outputs = [out_s.reshape(chans, rows, cols)]
    dconv_list = [dconv_s.reshape(chans, rows, cols)]
    output = jnp.stack(outputs)
    convolution_gradient = jnp.stack(dconv_list)
    d_conv_f = convolution_gradient.astype(jnp.float32)
    taps = []
    for row_tap in range(7):
        line = []
        for col_tap in range(7):
            line.append(
                jnp.sum(
                    d_conv_f
                    * extended[:, :, row_tap : row_tap + rows, col_tap : col_tap + cols].astype(
                        jnp.float32
                    ),
                    axis=(0, 2, 3),
                )
            )
        taps.append(jnp.stack(line, axis=1))
    g_depth = jnp.stack(taps, axis=1)
    lon_back = extended_2(convolution_gradient, (("lon", 3),), 3, True)
    band_back = extended_2(lon_back, (("lat", 2),), 3, False)
    deeper = jnp.pad(band_back, ((0, 0), (0, 0), (0, 3), (0, 0)))
    spread = jnp.zeros((samples, chans, rows + 3, cols), jnp.float32)
    for row_tap in range(7):
        for col_tap in range(7):
            spread = spread + weight_f[:, row_tap, col_tap][None, :, None, None] * deeper[
                :, :, 6 - row_tap : 9 - row_tap + rows, 6 - col_tap : 6 - col_tap + cols
            ].astype(jnp.float32)
    own = spread[:, :, :rows, :]
    margin = spread[:, :, rows:, :]
    back_init = jnp.zeros((samples, chans, 3, cols), jnp.float32)
    back = make_picker(
        own_partner,
        back_init,
        lax.all_gather(margin.astype(jnp.bfloat16), "lon", axis=3, tiled=True).astype(jnp.float32),
    )
    extra = back[:, :, ::-1, :]
    own = own.at[:, :, rows - 3 :, :].add(jnp.where(is_top, extra, 0.0))
    grad_fields = (mask_f[None, None] * cotangent.astype(jnp.float32) + own).astype(jnp.bfloat16)
    gain_gradient, g_bias, g_up_w, g_up_b, g_down, g_scale = parts
    summed = lax.psum(
        (g_depth, gain_gradient, g_bias, g_up_w, g_up_b, g_down, g_scale), ("lon", "lat")
    )
    return (
        output,
        grad_fields,
        summed[0],
        summed[1],
        summed[2],
        summed[3],
        summed[4],
        summed[5],
        summed[6],
    )


def solution(mesh):
    placed = (
        P(None, None, "lat", "lon"),
        P(None, None, "lat", "lon"),
        P("lat", "lon"),
        P(),
        P(),
        P(),
        P(),
        P(),
        P(),
        P(),
        P(),
    )
    return jax.shard_map(
        shards,
        mesh=mesh,
        in_specs=placed,
        out_specs=(
            P(None, None, "lat", "lon"),
            P(None, None, "lat", "lon"),
            P(),
            P(),
            P(),
            P(),
            P(),
            P(),
            P(),
        ),
        check_vma=False,
    )
```

profile of v0, /device:TPU:1, one launch (start us, length us, event | category | flops | bytes accessed | tf_op | source)
XLA Modules:
  0.0 497.8 jit_solution(14033838073368291433)
XLA Ops:
  10.5 7.2 %collective-permute-start = (bf16[1,64,16,3]{1,2,3,0:T(8,128)(2,1)S(1)}, bf16[1,64,16,3]{1,2,3,0:T(8,128)(2,1)S(1)}, u32[]{:S(2)}, u32[]{:S(2)}) collective-permute-start(bf16[1,64,16,3]{1,2,3,0:T(8,128)(2,1)S(1)} %get-tuple-element.147), channel_id=1, source_target_pairs={{0,16},{16,32},{32,48},{48,64},{64,80},{80,96},{96,112},{112,128},... | collective-permute-start | bytes 18440 | tf_op jit(solution)/shard_map/ppermute | solution.py:16
  17.7 3.5 collective-permute-start.1
  22.0 2.0 gather_fusion
  33.5 4.2 collective-permute-start.2
  37.7 42.1 %all-gather.3.cloned.1.call-done = bf16[1,64,3,4096]{3,1,2,0:T(8,128)(2,1)} async-done(((bf16[1,64,3,128]{3,1,2,0:T(8,128)(2,1)}), bf16[1,64,3,4096]{3,1,2,0:T(8,128)(2,1)}) %all-gather.3.cloned.1.call-update) | async-done | bytes 1572880 | tf_op jit(solution)/shard_map/all_gather | solution.py:116
  79.8 6.4 %copy.102 = bf16[1,64,3,4096]{1,2,3,0:T(4,128)(2,1)} copy(bf16[1,64,3,4096]{3,1,2,0:T(8,128)(2,1)} %all-gather.3.cloned.1.call-done) | data formatting | bytes 3145728 | tf_op jit(solution)/shard_map/all_gather | solution.py:116
  86.2 3.0 gather_fusion.1
  90.4 10.0 %fusion.134 = (f32[16,128]{0,1:T(8,128)S(1)}, f32[1,64,16,128]{1,2,3,0:T(8,128)S(1)}) fusion(bf16[1,64,19,134]{1,2,3,0:T(8,128)(2,1)S(1)} %get-tuple-element.142, f32[64]{0:T(128)S(1)} %get-tuple-element.152, f32[64]{0:T(128)S(1)} %get-tuple-element.153, f32[64]{0:T(128)S(1)} %get-tuple-element.154, f32[64]{0:T(128)S(1)} %get-tuple-element.155, ...), kind=kLoop, calls=%fused_computation.375 | loop fusion | flops 20051968 | bytes 11829504 | tf_op jit(solution)/shard_map/reduce_sum | solution.py:33
  102.8 6.9 %fusion.5 = (bf16[256,2048]{0,1:T(8,128)(2,1)}, f32[256,2048]{0,1:T(8,128)S(1)}) fusion(f32[256]{0:T(256)S(1)} %copy-done.99, bf16[256,64]{0,1:T(8,128)(2,1)S(1)} %copy-done, f32[64]{0:T(128)S(1)} %copy-done.94, f32[64]{0:T(128)S(1)} %copy-done.85, f32[2048]{0:T(1024)S(1)} %rsqrt_bitcast_fusion, f32[2048]{0:T(1024)S(1)} %get-tuple-element.202, ...), kind=kOutput, calls=%fused_computation.63 | convolution fusion | flops 102367232 | bytes 3720704 | tf_op jit(solution)/shard_map/dot_general | solution.py:43
  109.7 2.0 convert_reduce_fusion
  115.9 4.1 fusion.113
  120.2 3.2 collective-permute-start.4
  123.4 2.1 collective-permute-start.5
  127.1 7.3 %collective-permute-done.5 = bf16[1,64,16,3]{3,1,2,0:T(8,128)(2,1)S(1)} collective-permute-done((bf16[1,64,16,3]{3,1,2,0:T(8,128)(2,1)S(1)}, bf16[1,64,16,3]{3,1,2,0:T(8,128)(2,1)S(1)}, u32[]{:S(2)}, u32[]{:S(2)}) %collective-permute-start.5) | collective-permute-done | bytes 6176 | tf_op jit(solution)/shard_map/ppermute | solution.py:18
  135.2 1.9 collective-permute-start.6
  146.7 1.8 pad_maximum_fusion.2
  148.7 6.7 %multiply_add_fusion = f32[1,64,19,128]{3,1,2,0:T(8,128)S(1)} fusion(bf16[1,64,19,134]{3,1,2,0:T(8,128)(2,1)S(1)} %get-tuple-element.138, bf16[1,64,22,134]{3,1,2,0:T(8,128)(2,1)S(1)} %pad_maximum_fusion.1, bf16[1,64,19,134]{3,1,2,0:T(8,128)(2,1)S(1)} %get-tuple-element.137, f32[64]{0:T(128)S(1)} %copy-done.53, f32[64]{0:T(128)S(1)} %copy-done.55, ...), kind=kLoop, calls=%fused_computation.239 | loop fusion | flops 22724608 | bytes 10078720 | tf_op jit(solution)/shard_map/add | solution.py:164
  158.3 3.9 fusion.85
  166.1 2.3 fusion.133
  168.5 107.1 %all-reduce.1 = (f32[64,7,7]{0,2,1:T(8,128)}, f32[64]{0:T(128)}, f32[64]{0:T(128)}, f32[256]{0:T(256)}, f32[64]{0:T(128)}) all-reduce(f32[64,7,7]{0,2,1:T(8,128)S(1)} %constant_dynamic-update-slice_fusion, f32[64]{0:T(128)S(1)} %copy-done.92, f32[64]{0:T(128)S(1)} %copy-done.91, ...), channel_id=1, replica_groups=mesh['lon'=32,'lat'=16] {'lon','lat'}, use_global_device_ids=true, to_apply=%region_53.54 | all-reduce | flops 3584 | bytes 28672 | tf_op jit(solution)/shard_map/psum | solution.py:179
  275.6 6.4 %copy.112 = bf16[1,64,3,4096]{1,2,3,0:T(4,128)(2,1)} copy(bf16[1,64,3,4096]{3,1,2,0:T(8,128)(2,1)} %all-gather.5.cloned.1.call-done) | data formatting | bytes 3145728 | tf_op jit(solution)/shard_map/all_gather | solution.py:173
  282.1 6.3 %bitcast_convert_fusion = f32[64,3,4096]{0,1,2:T(4,128)} fusion(bf16[1,64,3,4096]{1,2,3,0:T(4,128)(2,1)} %copy.112), kind=kLoop, calls=%fused_computation.52 | loop fusion | flops 786432 | bytes 4718592 | tf_op jit(solution)/shard_map/convert_element_type | solution.py:173
  288.3 4.3 gather_fusion.2
  293.8 194.5 %all-reduce.5.cloned.1.call-done = (f32[256,64]{0,1:T(8,128)}, f32[64,256]{1,0:T(8,128)}) async-done(((f32[256,64]{0,1:T(8,128)}, f32[64,256]{1,0:T(8,128)}), (f32[256,64]{0,1:T(8,128)}, f32[64,256]{1,0:T(8,128)})) %all-reduce.5.cloned.1.call-update) | async-done | bytes 131088 | tf_op jit(solution)/shard_map/psum | solution.py:179
  (290 shorter events, 43.3 us)
Async XLA Ops:
  7.2 95.5 %copy-start = (bf16[256,64]{0,1:T(8,128)(2,1)S(1)}, bf16[256,64]{0,1:T(8,128)(2,1)}, u32[]{:S(2)}) copy-start(bf16[256,64]{0,1:T(8,128)(2,1)} %param.20) | copy-start | bytes 98308
  7.2 72.6 %all-gather.3.cloned.1.call-start = ((), (), s32[]{:S(2)}) async-start(), calls=%async_computation | async-start | bytes 1622016 | tf_op jit(solution)/shard_map/all_gather | solution.py:116
  8.9 266.7 %all-gather.5.cloned.1.call-start = ((), (), s32[]{:S(2)}) async-start(), calls=%async_computation.1 | async-start | bytes 1622016 | tf_op jit(solution)/shard_map/all_gather | solution.py:173
  10.5 16.3 %collective-permute-start = (bf16[1,64,16,3]{1,2,3,0:T(8,128)(2,1)S(1)}, bf16[1,64,16,3]{1,2,3,0:T(8,128)(2,1)S(1)}, u32[]{:S(2)}, u32[]{:S(2)}) collective-permute-start(bf16[1,64,16,3]{1,2,3,0:T(8,128)(2,1)S(1)} %get-tuple-element.147), channel_id=1, source_target_pairs={{0,16},{16,32},{32,48},{48,64},{64,80},{80,96},{96,112},{112,128},... | collective-permute-start | bytes 18440 | tf_op jit(solution)/shard_map/ppermute | solution.py:16
  17.7 9.1 %collective-permute-start.1 = (bf16[1,64,16,3]{1,2,3,0:T(8,128)(2,1)S(1)}, bf16[1,64,16,3]{1,2,3,0:T(8,128)(2,1)S(1)}, u32[]{:S(2)}, u32[]{:S(2)}) collective-permute-start(bf16[1,64,16,3]{1,2,3,0:T(8,128)(2,1)S(1)} %get-tuple-element.148), channel_id=1, source_target_pairs={{16,0},{32,16},{48,32},{64,48},{80,64},{96,80},{112,96},{128,112},... | collective-permute-start | bytes 18440 | tf_op jit(solution)/shard_map/ppermute | solution.py:18
  24.7 65.4 %copy-start.28 = (f32[64]{0:T(128)}, f32[64]{0:T(128)S(1)}, u32[]{:S(2)}) copy-start(f32[64]{0:T(128)S(1)} %get-tuple-element.189) | copy-start | bytes 772
  24.7 65.4 %copy-start.30 = (f32[64]{0:T(128)}, f32[64]{0:T(128)S(1)}, u32[]{:S(2)}) copy-start(f32[64]{0:T(128)S(1)} %get-tuple-element.190) | copy-start | bytes 772
  24.7 65.4 %copy-start.32 = (f32[64]{0:T(128)}, f32[64]{0:T(128)S(1)}, u32[]{:S(2)}) copy-start(f32[64]{0:T(128)S(1)} %get-tuple-element.191) | copy-start | bytes 772
  24.7 65.4 %copy-start.34 = (f32[64]{0:T(128)}, f32[64]{0:T(128)S(1)}, u32[]{:S(2)}) copy-start(f32[64]{0:T(128)S(1)} %get-tuple-element.192) | copy-start | bytes 772
  24.7 65.4 %copy-start.36 = (f32[64]{0:T(128)}, f32[64]{0:T(128)S(1)}, u32[]{:S(2)}) copy-start(f32[64]{0:T(128)S(1)} %get-tuple-element.193) | copy-start | bytes 772
  24.7 65.4 %copy-start.38 = (f32[64]{0:T(128)}, f32[64]{0:T(128)S(1)}, u32[]{:S(2)}) copy-start(f32[64]{0:T(128)S(1)} %get-tuple-element.194) | copy-start | bytes 772
  24.7 65.4 %copy-start.40 = (f32[64]{0:T(128)}, f32[64]{0:T(128)S(1)}, u32[]{:S(2)}) copy-start(f32[64]{0:T(128)S(1)} %get-tuple-element.195) | copy-start | bytes 772
  24.8 65.4 %copy-start.42 = (f32[64]{0:T(128)}, f32[64]{0:T(128)S(1)}, u32[]{:S(2)}) copy-start(f32[64]{0:T(128)S(1)} %get-tuple-element.196) | copy-start | bytes 772
  24.8 65.4 %copy-start.44 = (f32[64]{0:T(128)}, f32[64]{0:T(128)S(1)}, u32[]{:S(2)}) copy-start(f32[64]{0:T(128)S(1)} %get-tuple-element.197) | copy-start | bytes 772
  24.8 65.4 %copy-start.46 = (f32[64]{0:T(128)}, f32[64]{0:T(128)S(1)}, u32[]{:S(2)}) copy-start(f32[64]{0:T(128)S(1)} %get-tuple-element.198) | copy-start | bytes 772
  24.8 65.4 %copy-start.48 = (f32[64]{0:T(128)}, f32[64]{0:T(128)S(1)}, u32[]{:S(2)}) copy-start(f32[64]{0:T(128)S(1)} %get-tuple-element.199) | copy-start | bytes 772
  26.8 82.9 %copy-start.18 = (f32[2048]{0:T(1024)}, f32[2048]{0:T(1024)S(1)}, u32[]{:S(2)}) copy-start(f32[2048]{0:T(1024)S(1)} %get-tuple-element.201) | copy-start | bytes 24580
  27.0 62.2 %collective-permute-start.3 = (bf16[1,64,3,134]{1,2,3,0:T(4,128)(2,1)S(1)}, bf16[1,64,3,134]{1,2,3,0:T(4,128)(2,1)S(1)}, u32[]{:S(2)}, u32[]{:S(2)}) collective-permute-start(bf16[1,64,3,134]{1,2,3,0:T(4,128)(2,1)S(1)} %get-tuple-element.144), channel_id=1, source_target_pairs={{1,0},{2,1},{3,2},{4,3},{5,4},{6,5},{7,6},{8,7},{9,8},{10,9},{11,1... | collective-permute-start | bytes 154376 | tf_op jit(solution)/shard_map/ppermute | solution.py:18
  33.5 56.1 %collective-permute-start.2 = (bf16[1,64,3,134]{1,2,3,0:T(4,128)(2,1)S(1)}, bf16[1,64,3,134]{1,2,3,0:T(4,128)(2,1)S(1)}, u32[]{:S(2)}, u32[]{:S(2)}) collective-permute-start(bf16[1,64,3,134]{1,2,3,0:T(4,128)(2,1)S(1)} %get-tuple-element.143), channel_id=1, source_target_pairs={{0,1},{1,2},{2,3},{3,4},{4,5},{5,6},{6,7},{7,8},{8,9},{9,10},{10,1... | collective-permute-start | bytes 154376 | tf_op jit(solution)/shard_map/ppermute | solution.py:16
  120.2 6.9 %collective-permute-start.4 = (bf16[1,64,16,3]{3,1,2,0:T(8,128)(2,1)S(1)}, bf16[1,64,16,3]{3,1,2,0:T(8,128)(2,1)S(1)}, u32[]{:S(2)}, u32[]{:S(2)}) collective-permute-start(bf16[1,64,16,3]{3,1,2,0:T(8,128)(2,1)S(1)} %get-tuple-element.149), channel_id=1, source_target_pairs={{0,16},{16,32},{32,48},{48,64},{64,80},{80,96},{96,112},{112,128},... | collective-permute-start | bytes 18440 | tf_op jit(solution)/shard_map/ppermute | solution.py:16
  123.4 11.0 %collective-permute-start.5 = (bf16[1,64,16,3]{3,1,2,0:T(8,128)(2,1)S(1)}, bf16[1,64,16,3]{3,1,2,0:T(8,128)(2,1)S(1)}, u32[]{:S(2)}, u32[]{:S(2)}) collective-permute-start(bf16[1,64,16,3]{3,1,2,0:T(8,128)(2,1)S(1)} %get-tuple-element.150), channel_id=1, source_target_pairs={{16,0},{32,16},{48,32},{64,48},{80,64},{96,80},{112,96},{128,112},... | collective-permute-start | bytes 18440 | tf_op jit(solution)/shard_map/ppermute | solution.py:18
  135.2 10.0 %collective-permute-start.6 = (bf16[1,64,3,134]{3,1,2,0:T(8,128)(2,1)}, bf16[1,64,3,134]{3,1,2,0:T(8,128)(2,1)}, u32[]{:S(2)}, u32[]{:S(2)}) collective-permute-start(bf16[1,64,3,134]{3,1,2,0:T(8,128)(2,1)} %get-tuple-element.140), channel_id=1, source_target_pairs={{0,1},{1,2},{2,3},{3,4},{4,5},{5,6},{6,7},{7,8},{8,9},{9,10},{10,1... | collective-permute-start | bytes 154376 | tf_op jit(solution)/shard_map/ppermute | solution.py:16
  137.2 8.1 %collective-permute-start.7 = (bf16[1,64,3,134]{3,1,2,0:T(8,128)(2,1)}, bf16[1,64,3,134]{3,1,2,0:T(8,128)(2,1)}, u32[]{:S(2)}, u32[]{:S(2)}) collective-permute-start(bf16[1,64,3,134]{3,1,2,0:T(8,128)(2,1)} %get-tuple-element.139), channel_id=1, source_target_pairs={{1,0},{2,1},{3,2},{4,3},{5,4},{6,5},{7,6},{8,7},{9,8},{10,9},{11,1... | collective-permute-start | bytes 154376 | tf_op jit(solution)/shard_map/ppermute | solution.py:18
  156.9 331.4 %all-reduce.5.cloned.1.call-start = ((), (), s32[]{:S(2)}) async-start(), calls=%async_computation.2 | async-start | bytes 262144 | tf_op jit(solution)/shard_map/psum | solution.py:179
  (88 other events, 1441.2 us)
Sparse Core Ops, SparseCore 0:
  11.7 68.0 all-gather.2
  157.0 65.3 all-gather.4
  228.2 260.0 all-reduce.4
where the time goes:
time: 499 us; the launch traced here: 498 us
  waiting for transfers between devices  244 us (49%)
  blocking collectives  107 us (21%)
  local copies, waits for them, and re-layouts  46.1 us (9%)
  other arithmetic  45.4 us (9%)
  starting transfers between devices  24.7 us (5%)
  between operations  15.4 us (3%)
  matrix products  15.1 us (3%)
    psum x1, waiting for transfers between devices, shards(): lax.psum((g_depth, gain_gradient, g_bias, g_up_w, g_up_b, g_down, g_scale...  195 us
    psum x1, blocking collectives, shards(): lax.psum((g_depth, gain_gradient, g_bias, g_up_w, g_up_b, g_down, g_scale...  107 us
    all_gather x1, waiting for transfers between devices, shards(): lax.all_gather(upper, 'lon', axis=3, tiled=True)  42.1 us
    ppermute x4, starting transfers between devices, extended_2(): lax.ppermute(tail, axis, [(i, (i + 1) % count) for i in range(ends)])  16.4 us
    reduce_sum x4, other arithmetic, shards(): jnp.sum(d_conv_f * extended[:, :, row_tap:row_tap + rows, col_tap:col_tap...  10.9 us
    reduce_sum x1, other arithmetic, cell_terms(): mean_c = jnp.mean(conv, axis=0, keepdims=True)  9.98 us
  transfers between devices with their start and end apart: 11, of which 3 were waited for; matrix products, arithmetic and copies ran while one was open for 12% of the time, Pallas kernels for 0%

commit v1 on v0

--- a/solution.py
+++ b/solution.py
@@ -176,9 +176,8 @@
     own = own.at[:, :, rows - 3 :, :].add(jnp.where(is_top, extra, 0.0))
     grad_fields = (mask_f[None, None] * cotangent.astype(jnp.float32) + own).astype(jnp.bfloat16)
     gain_gradient, g_bias, g_up_w, g_up_b, g_down, g_scale = parts
-    summed = lax.psum(
-        (g_depth, gain_gradient, g_bias, g_up_w, g_up_b, g_down, g_scale), ("lon", "lat")
-    )
+    partial = lax.psum((g_depth, gain_gradient, g_bias, g_up_w, g_up_b, g_down, g_scale), "lat")
+    summed = lax.psum(partial, "lon")
     return (
         output,
         grad_fields,

time: 499 us -> 643 us (1.29)
  blocking collectives: 107 us -> 199 us
  waiting for transfers between devices: 244 us -> 304 us
  local copies, waits for them, and re-layouts: 46.1 us -> 39 us
    psum x0 -> x1, waiting for transfers between devices: none -> 250 us  [shards(): summed = lax.psum(partial, 'lon')]
    psum x1, waiting for transfers between devices: 195 us -> 0.01 us  [shards(): lax.psum((g_depth, gain_gradient, g_bias, g_up_w, g_up_b, g_down, g_scale...]
    psum x0 -> x1, blocking collectives: none -> 149 us  [shards(): summed = lax.psum(partial, 'lon')]
    psum x1, blocking collectives: 107 us -> 50.3 us  [shards(): lax.psum((g_depth, gain_gradient, g_bias, g_up_w, g_up_b, g_down, g_scale...]
  transfers between devices with their start and end apart: 11 -> 12, of which waited for: 3 -> 5; matrix products, arithmetic and copies ran while one was open for 12% -> 9% of each run, Pallas kernels for 0% -> 0%
where the time goes in v1:
time: 643 us; the launch traced here: 642 us
  waiting for transfers between devices  304 us (47%)
  blocking collectives  199 us (31%)
  other arithmetic  44.5 us (7%)
  local copies, waits for them, and re-layouts  39 us (6%)
  starting transfers between devices  24.9 us (4%)
  matrix products  15.7 us (2%)
  between operations  15.4 us (2%)
    psum x1, waiting for transfers between devices, shards(): summed = lax.psum(partial, 'lon')  250 us
    psum x1, blocking collectives, shards(): summed = lax.psum(partial, 'lon')  149 us
    psum x1, blocking collectives, shards(): lax.psum((g_depth, gain_gradient, g_bias, g_up_w, g_up_b, g_down, g_scale...  50.3 us
    all_gather x1, waiting for transfers between devices, shards(): lax.all_gather(upper, 'lon', axis=3, tiled=True)  42.4 us
    ppermute x4, starting transfers between devices, extended_2(): lax.ppermute(tail, axis, [(i, (i + 1) % count) for i in range(ends)])  16.7 us
  transfers between devices with their start and end apart: 12, of which 5 were waited for; matrix products, arithmetic and copies ran while one was open for 9% of the time, Pallas kernels for 0%

profile of v1, /device:TPU:1, one launch (start us, length us, event | category | flops | bytes accessed | tf_op | source)
XLA Modules:
  0.0 642.2 jit_solution(14889142366612477725)
XLA Ops:
  10.5 7.2 %collective-permute-start = (bf16[1,64,16,3]{1,2,3,0:T(8,128)(2,1)S(1)}, bf16[1,64,16,3]{1,2,3,0:T(8,128)(2,1)S(1)}, u32[]{:S(2)}, u32[]{:S(2)}) collective-permute-start(bf16[1,64,16,3]{1,2,3,0:T(8,128)(2,1)S(1)} %get-tuple-element.154), channel_id=1, source_target_pairs={{0,16},{16,32},{32,48},{48,64},{64,80},{80,96},{96,112},{112,128},... | collective-permute-start | bytes 18440 | tf_op jit(solution)/shard_map/ppermute | solution.py:16
  17.7 3.5 collective-permute-start.1
  22.0 2.0 gather_fusion
  32.5 4.2 collective-permute-start.2
  36.7 42.4 %all-gather.3.cloned.1.call-done = bf16[1,64,3,4096]{3,1,2,0:T(8,128)(2,1)} async-done(((bf16[1,64,3,128]{3,1,2,0:T(8,128)(2,1)}), bf16[1,64,3,4096]{3,1,2,0:T(8,128)(2,1)}) %all-gather.3.cloned.1.call-update) | async-done | bytes 1572880 | tf_op jit(solution)/shard_map/all_gather | solution.py:116
  79.1 6.4 copy.102
  85.5 3.0 gather_fusion.1
  89.7 10.5 %fusion.134 = (f32[16,128]{0,1:T(8,128)S(1)}, f32[1,64,16,128]{1,2,3,0:T(8,128)S(1)}) fusion(bf16[1,64,19,134]{1,2,3,0:T(8,128)(2,1)S(1)} %get-tuple-element.149, f32[64]{0:T(128)S(1)} %get-tuple-element.159, f32[64]{0:T(128)S(1)} %get-tuple-element.160, f32[64]{0:T(128)S(1)} %get-tuple-element.161, f32[64]{0:T(128)S(1)} %get-tuple-element.162, ...), kind=kLoop, calls=%fused_computation.375 | loop fusion | flops 20051968 | bytes 11829504 | tf_op jit(solution)/shard_map/reduce_sum | solution.py:33
  102.5 6.9 %fusion.5 = (bf16[256,2048]{0,1:T(8,128)(2,1)}, f32[256,2048]{0,1:T(8,128)S(1)}) fusion(f32[256]{0:T(256)S(1)} %convert_element_type.474, bf16[256,64]{0,1:T(8,128)(2,1)S(1)} %copy-done, f32[64]{0:T(128)} %convert_element_type.472, f32[64]{0:T(128)} %convert_element_type.471, f32[2048]{0:T(1024)S(1)} %rsqrt_bitcast_fusion, ...), kind=kOutput, calls=%fused_computation.63 | convolution fusion | flops 102367232 | bytes 3720704 | tf_op jit(solution)/shard_map/dot_general | solution.py:43
  109.5 2.0 convert_reduce_fusion
  116.6 4.4 fusion.113
  121.2 3.3 collective-permute-start.4
  128.2 7.2 %collective-permute-done.5 = bf16[1,64,16,3]{3,1,2,0:T(8,128)(2,1)S(1)} collective-permute-done((bf16[1,64,16,3]{3,1,2,0:T(8,128)(2,1)S(1)}, bf16[1,64,16,3]{3,1,2,0:T(8,128)(2,1)S(1)}, u32[]{:S(2)}, u32[]{:S(2)}) %collective-permute-start.5) | collective-permute-done | bytes 6176 | tf_op jit(solution)/shard_map/ppermute | solution.py:18
  136.2 2.1 collective-permute-start.6
  140.7 4.2 collective-permute-done.7
  147.8 7.0 %multiply_add_fusion = f32[1,64,19,128]{3,1,2,0:T(8,128)S(1)} fusion(bf16[1,64,19,134]{3,1,2,0:T(8,128)(2,1)S(1)} %get-tuple-element.145, bf16[1,64,22,134]{3,1,2,0:T(8,128)(2,1)S(1)} %pad_maximum_fusion.1, bf16[1,64,19,134]{3,1,2,0:T(8,128)(2,1)S(1)} %get-tuple-element.144, f32[64]{0:T(128)} %copy-done.38, f32[64]{0:T(128)} %copy-done.39, ...), kind=kLoop, calls=%fused_computation.239 | loop fusion | flops 22724608 | bytes 10072832 | tf_op jit(solution)/shard_map/add | solution.py:164
  156.3 2.2 multiply_reduce_fusion.1
  162.2 3.3 fusion.85
  165.7 50.3 %all-reduce.3 = (f32[64,7,7]{0,2,1:T(8,128)S(1)}, f32[64]{0:T(128)S(1)}, f32[64]{0:T(128)S(1)}, f32[256]{0:T(256)S(1)}, f32[64]{0:T(128)S(1)}) all-reduce(f32[64,7,7]{0,2,1:T(8,128)S(1)} %constant_dynamic-update-slice_fusion, f32[64]{0:T(128)S(1)} %copy-done.87, f32[64]{0:T(128)S(1)} %reduce_sum.567, ...), channel_id=1, replica_groups=mesh['lon'=32,'lat'=16] {'lat'}, use_global_device_ids=true, to_apply=%region_53.54 | all-reduce | flops 3584 | bytes 28672 | tf_op jit(solution)/shard_map/psum | solution.py:179
  216.0 148.8 %all-reduce.1 = (f32[64,7,7]{0,2,1:T(8,128)}, f32[64]{0:T(128)}, f32[64]{0:T(128)}, f32[256]{0:T(256)}, f32[64]{0:T(128)}) all-reduce(f32[64,7,7]{0,2,1:T(8,128)S(1)} %get-tuple-element.131, f32[64]{0:T(128)S(1)} %get-tuple-element.132, f32[64]{0:T(128)S(1)} %get-tuple-element.133, ...), channel_id=1, replica_groups=mesh['lon'=32,'lat'=16] {'lon'}, use_global_device_ids=true, to_apply=%region_54.55 | all-reduce | flops 3584 | bytes 28672 | tf_op jit(solution)/shard_map/psum | solution.py:180
  364.8 6.4 copy.112
  371.3 6.2 bitcast_convert_fusion
  377.5 4.3 gather_fusion.2
  383.0 249.8 %all-reduce.8.cloned.1.call-done = (f32[256,64]{0,1:T(8,128)}, f32[64,256]{1,0:T(8,128)}) async-done(((f32[256,64]{0,1:T(8,128)}, f32[64,256]{1,0:T(8,128)}), (f32[256,64]{0,1:T(8,128)}, f32[64,256]{1,0:T(8,128)})) %all-reduce.8.cloned.1.call-update) | async-done | bytes 131088 | tf_op jit(solution)/shard_map/psum | solution.py:180
  (280 shorter events, 39.4 us)
Async XLA Ops:
  7.2 95.3 %copy-start = (bf16[256,64]{0,1:T(8,128)(2,1)S(1)}, bf16[256,64]{0,1:T(8,128)(2,1)}, u32[]{:S(2)}) copy-start(bf16[256,64]{0,1:T(8,128)(2,1)} %param.20) | copy-start | bytes 98308
  7.2 71.9 %all-gather.3.cloned.1.call-start = ((), (), s32[]{:S(2)}) async-start(), calls=%async_computation | async-start | bytes 1622016 | tf_op jit(solution)/shard_map/all_gather | solution.py:116
  8.9 355.9 %all-reduce.10.cloned.1.call-start = ((), (), s32[]{:S(2)}) async-start(), calls=%async_computation.3 | async-start | bytes 262144 | tf_op jit(solution)/shard_map/psum | solution.py:179
  10.5 15.9 %collective-permute-start = (bf16[1,64,16,3]{1,2,3,0:T(8,128)(2,1)S(1)}, bf16[1,64,16,3]{1,2,3,0:T(8,128)(2,1)S(1)}, u32[]{:S(2)}, u32[]{:S(2)}) collective-permute-start(bf16[1,64,16,3]{1,2,3,0:T(8,128)(2,1)S(1)} %get-tuple-element.154), channel_id=1, source_target_pairs={{0,16},{16,32},{32,48},{48,64},{64,80},{80,96},{96,112},{112,128},... | collective-permute-start | bytes 18440 | tf_op jit(solution)/shard_map/ppermute | solution.py:16
  17.7 8.7 %collective-permute-start.1 = (bf16[1,64,16,3]{1,2,3,0:T(8,128)(2,1)S(1)}, bf16[1,64,16,3]{1,2,3,0:T(8,128)(2,1)S(1)}, u32[]{:S(2)}, u32[]{:S(2)}) collective-permute-start(bf16[1,64,16,3]{1,2,3,0:T(8,128)(2,1)S(1)} %get-tuple-element.155), channel_id=1, source_target_pairs={{16,0},{32,16},{48,32},{64,48},{80,64},{96,80},{112,96},{128,112},... | collective-permute-start | bytes 18440 | tf_op jit(solution)/shard_map/ppermute | solution.py:18
  24.7 64.6 %copy-start.24 = (f32[64]{0:T(128)}, f32[64]{0:T(128)S(1)}, u32[]{:S(2)}) copy-start(f32[64]{0:T(128)S(1)} %get-tuple-element.196) | copy-start | bytes 772
  24.7 64.6 %copy-start.26 = (f32[64]{0:T(128)}, f32[64]{0:T(128)S(1)}, u32[]{:S(2)}) copy-start(f32[64]{0:T(128)S(1)} %get-tuple-element.197) | copy-start | bytes 772
  24.7 64.6 %copy-start.28 = (f32[64]{0:T(128)}, f32[64]{0:T(128)S(1)}, u32[]{:S(2)}) copy-start(f32[64]{0:T(128)S(1)} %get-tuple-element.198) | copy-start | bytes 772
  24.7 64.6 %copy-start.29 = (f32[64]{0:T(128)}, f32[64]{0:T(128)S(1)}, u32[]{:S(2)}) copy-start(f32[64]{0:T(128)S(1)} %get-tuple-element.199) | copy-start | bytes 772
  24.7 64.6 %copy-start.30 = (f32[64]{0:T(128)}, f32[64]{0:T(128)S(1)}, u32[]{:S(2)}) copy-start(f32[64]{0:T(128)S(1)} %get-tuple-element.200) | copy-start | bytes 772
  24.7 64.6 %copy-start.31 = (f32[64]{0:T(128)}, f32[64]{0:T(128)S(1)}, u32[]{:S(2)}) copy-start(f32[64]{0:T(128)S(1)} %get-tuple-element.201) | copy-start | bytes 772
  24.8 64.6 %copy-start.32 = (f32[64]{0:T(128)}, f32[64]{0:T(128)S(1)}, u32[]{:S(2)}) copy-start(f32[64]{0:T(128)S(1)} %get-tuple-element.202) | copy-start | bytes 772
  24.8 64.6 %copy-start.33 = (f32[64]{0:T(128)}, f32[64]{0:T(128)S(1)}, u32[]{:S(2)}) copy-start(f32[64]{0:T(128)S(1)} %get-tuple-element.203) | copy-start | bytes 772
  24.8 64.6 %copy-start.34 = (f32[64]{0:T(128)}, f32[64]{0:T(128)S(1)}, u32[]{:S(2)}) copy-start(f32[64]{0:T(128)S(1)} %get-tuple-element.204) | copy-start | bytes 772
  24.8 64.6 %copy-start.35 = (f32[64]{0:T(128)}, f32[64]{0:T(128)S(1)}, u32[]{:S(2)}) copy-start(f32[64]{0:T(128)S(1)} %get-tuple-element.205) | copy-start | bytes 772
  24.8 64.6 %copy-start.36 = (f32[64]{0:T(128)}, f32[64]{0:T(128)S(1)}, u32[]{:S(2)}) copy-start(f32[64]{0:T(128)S(1)} %get-tuple-element.206) | copy-start | bytes 772
  26.6 61.8 %collective-permute-start.3 = (bf16[1,64,3,134]{1,2,3,0:T(4,128)(2,1)S(1)}, bf16[1,64,3,134]{1,2,3,0:T(4,128)(2,1)S(1)}, u32[]{:S(2)}, u32[]{:S(2)}) collective-permute-start(bf16[1,64,3,134]{1,2,3,0:T(4,128)(2,1)S(1)} %get-tuple-element.151), channel_id=1, source_target_pairs={{1,0},{2,1},{3,2},{4,3},{5,4},{6,5},{7,6},{8,7},{9,8},{10,9},{11,1... | collective-permute-start | bytes 154376 | tf_op jit(solution)/shard_map/ppermute | solution.py:18
  32.5 56.3 %collective-permute-start.2 = (bf16[1,64,3,134]{1,2,3,0:T(4,128)(2,1)S(1)}, bf16[1,64,3,134]{1,2,3,0:T(4,128)(2,1)S(1)}, u32[]{:S(2)}, u32[]{:S(2)}) collective-permute-start(bf16[1,64,3,134]{1,2,3,0:T(4,128)(2,1)S(1)} %get-tuple-element.150), channel_id=1, source_target_pairs={{0,1},{1,2},{2,3},{3,4},{4,5},{5,6},{6,7},{7,8},{8,9},{9,10},{10,1... | collective-permute-start | bytes 154376 | tf_op jit(solution)/shard_map/ppermute | solution.py:16
  121.2 7.0 %collective-permute-start.4 = (bf16[1,64,16,3]{3,1,2,0:T(8,128)(2,1)S(1)}, bf16[1,64,16,3]{3,1,2,0:T(8,128)(2,1)S(1)}, u32[]{:S(2)}, u32[]{:S(2)}) collective-permute-start(bf16[1,64,16,3]{3,1,2,0:T(8,128)(2,1)S(1)} %get-tuple-element.156), channel_id=1, source_target_pairs={{0,16},{16,32},{32,48},{48,64},{64,80},{80,96},{96,112},{112,128},... | collective-permute-start | bytes 18440 | tf_op jit(solution)/shard_map/ppermute | solution.py:16
  124.5 10.9 %collective-permute-start.5 = (bf16[1,64,16,3]{3,1,2,0:T(8,128)(2,1)S(1)}, bf16[1,64,16,3]{3,1,2,0:T(8,128)(2,1)S(1)}, u32[]{:S(2)}, u32[]{:S(2)}) collective-permute-start(bf16[1,64,16,3]{3,1,2,0:T(8,128)(2,1)S(1)} %get-tuple-element.157), channel_id=1, source_target_pairs={{16,0},{32,16},{48,32},{64,48},{80,64},{96,80},{112,96},{128,112},... | collective-permute-start | bytes 18440 | tf_op jit(solution)/shard_map/ppermute | solution.py:18
  136.2 4.5 collective-permute-start.6
  138.2 6.6 %collective-permute-start.7 = (bf16[1,64,3,134]{3,1,2,0:T(8,128)(2,1)}, bf16[1,64,3,134]{3,1,2,0:T(8,128)(2,1)}, u32[]{:S(2)}, u32[]{:S(2)}) collective-permute-start(bf16[1,64,3,134]{3,1,2,0:T(8,128)(2,1)} %get-tuple-element.146), channel_id=1, source_target_pairs={{1,0},{2,1},{3,2},{4,3},{5,4},{6,5},{7,6},{8,7},{9,8},{10,9},{11,1... | collective-permute-start | bytes 154376 | tf_op jit(solution)/shard_map/ppermute | solution.py:18
  140.6 224.2 %all-gather.5.cloned.1.call-start = ((), (), s32[]{:S(2)}) async-start(), calls=%async_computation.1 | async-start | bytes 1622016 | tf_op jit(solution)/shard_map/all_gather | solution.py:173
  156.3 476.5 %all-reduce.8.cloned.1.call-start = ((), (), s32[]{:S(2)}) async-start(), calls=%async_computation.2 | async-start | bytes 262144 | tf_op jit(solution)/shard_map/psum | solution.py:180
  (82 other events, 2188.4 us)
Sparse Core Ops, SparseCore 0:
  11.7 67.3 all-gather.2
  140.7 135.3 all-reduce.9
  280.2 70.2 all-gather.4
  364.9 267.7 all-reduce.7
